TPU v7x, 128 devices: a whole 4x4x4 slice. The times are simulated.
128 devices in a mesh: row: 8 (over z, core), col: 16 (over y, x).
Axes of the slice: x: 4, y: 4, z: 4, core: 2. Of those that a mesh axis runs over, the one named last changes fastest.
Arguments:
- image: float32 [32, 32, 64, 128], P('row', 'col'), may hold values from -6 to 6
- u_factors: bfloat16 [40, 64, 1024, 256], P('row', 'col'), may hold values from -0.0625 to 0.0625
- v_factors: bfloat16 [40, 64, 1024, 256], P('row', 'col'), may hold values from -0.1875 to 0.1875
- ranks: int32 [40, 64], P('row', 'col'), may hold values from 16 to 256
- measured: bfloat16 [40960, 128], P('row'), may hold values from -6 to 6
Outputs:
- new_image: float32 [32, 32, 64, 128], P('row', 'col')
All inputs are finite; a program needn't handle non-finite values.
Results may differ from a plain program's by a relative error of at most 0.0051.
Values may be sent and summed in bfloat16 or wider, within the bound.
A program may use at most 128 MiB of HBM per device.

v0:
```python
import jax
import jax.numpy as jnp
from jax import lax
from jax.sharding import PartitionSpec as P

diff_rate = 0.12
edge_scale = 0.5


def padded_2(block, sides, width):
    for axis, dim in sides:
        count = lax.axis_size(axis)
        forward = [(i, i + 1) for i in range(count - 1)]
        backward = [(target, source) for source, target in forward]
        low = lax.ppermute(
            lax.slice_in_dim(block, block.shape[dim] - width, None, axis=dim), axis, forward
        )
        high = lax.ppermute(lax.slice_in_dim(block, 0, width, axis=dim), axis, backward)
        block = jnp.concatenate([low, block, high], axis=dim)
    return block


def flux(delta):
    scaled = delta / edge_scale
    return delta / (1.0 + scaled * scaled)


def diffuse_margin(extended):
    padded = jnp.pad(extended, ((0, 0), (0, 0), (1, 1), (0, 0)))
    center = padded[1:-1, 1:-1, 1:-1]
    total = flux(padded[2:, 1:-1, 1:-1] - center) + flux(padded[:-2, 1:-1, 1:-1] - center)
    total = total + flux(padded[1:-1, 2:, 1:-1] - center) + flux(padded[1:-1, :-2, 1:-1] - center)
    total = total + flux(padded[1:-1, 1:-1, 2:] - center) + flux(padded[1:-1, 1:-1, :-2] - center)
    return center + diff_rate * total


def body(image, u_factors, v_factors, ranks, measured):
    row_tiles, col_tiles, tile_len, rank_max = u_factors.shape
    frames = image.shape[3]
    whole = lax.all_gather(image.astype(jnp.bfloat16), "row", axis=0, tiled=True)
    xtiles = whole.reshape(col_tiles, tile_len, frames)
    levels = lax.broadcasted_iota(jnp.int32, (row_tiles, col_tiles, rank_max), 2)
    mask = (levels < ranks[:, :, None]).astype(jnp.float32)
    coef = jnp.einsum("ijkr,jkf->ijrf", v_factors, xtiles, preferred_element_type=jnp.float32)
    coef = (coef * mask[:, :, :, None]).astype(jnp.bfloat16)
    partial_value = jnp.einsum(
        "ijkr,ijrf->ikf", u_factors, coef, preferred_element_type=jnp.float32
    )
    partial_value = partial_value.reshape(row_tiles * tile_len, frames)
    total = lax.psum(partial_value, "col")
    resid = (total - measured.astype(jnp.float32)).astype(jnp.bfloat16)
    resid = resid.reshape(row_tiles, tile_len, frames)
    back = jnp.einsum("ijkr,ikf->ijrf", u_factors, resid, preferred_element_type=jnp.float32)
    back = (back * mask[:, :, :, None]).astype(jnp.bfloat16)
    grad_terms = jnp.einsum("ijkr,ijrf->jkf", v_factors, back, preferred_element_type=jnp.float32)
    grad_terms = grad_terms.reshape(col_tiles * tile_len, frames)
    gradient = lax.psum_scatter(grad_terms, "row", scatter_dimension=0, tiled=True)
    moved = image - gradient.reshape(image.shape)
    for step in range(2):
        extended = padded_2(moved, (("row", 0), ("col", 1)), 1)
        moved = diffuse_margin(extended)
    return moved


def solution(mesh):
    placed = (
        P("row", "col", None, None),
        P("row", "col", None, None),
        P("row", "col", None, None),
        P("row", "col"),
        P("row", None),
    )
    return jax.shard_map(
        body, mesh=mesh, in_specs=placed, out_specs=P("row", "col", None, None), check_vma=False
    )
```

profile of v0, /device:TPU:25, one launch (start us, length us, event | category | flops | bytes accessed | tf_op | source)
XLA Modules:
  0.0 237.7 jit_solution(13111002786819206620)
XLA Ops:
  6.5 0.0 all-gather.2.cloned.1.call-start
  6.5 1.6 convert_element_type.28
  8.2 0.0 all-gather.2.cloned.1.call-update
  8.2 0.0 all-reduce.4.cloned.1.call-start
  8.2 0.8 copy.20
  9.0 0.1 fusion.25
  9.1 26.1 %all-gather.2.cloned.1.call-done = bf16[32,2,64,128]{3,2,1,0:T(8,128)(2,1)} async-done(((bf16[4,2,64,128]{3,2,1,0:T(8,128)(2,1)}), bf16[32,2,64,128]{3,2,1,0:T(8,128)(2,1)}) %all-gather.2.cloned.1.call-update) | async-done | bytes 1048592 | tf_op jit(solution)/shard_map/all_gather | solution.py:40
  35.2 11.8 %convolution_bitcast_fusion = f32[5,1024,128]{1,2,0:T(8,128)S(1)} fusion(bf16[5,4,1024,256]{3,2,1,0:T(8,128)(2,1)} %param.6, bf16[4,1024,128,1]{2,1,0,3:T(8,128)(2,1)} %bitcast.33, bf16[5,4,1024,256]{3,2,1,0:T(8,128)(2,1)} %param.7, f32[5,4,256]{2,1,0:T(4,128)S(1)} %fusion.25), kind=kOutput, calls=%fused_computation.8 | convolution fusion | flops 2685665280 | bytes 24662016 | tf_op jit(solution)/shard_map/ijkr,ijrf->ikf/dot_general | solution.py:46
  47.0 2.1 copy.21
  49.1 0.0 copy-start
  49.1 0.0 all-reduce.4.cloned.1.call-update
  49.2 0.0 reduce-scatter.2.cloned.1.call-start
  49.2 90.6 %all-reduce.4.cloned.1.call-done = f32[5120,128]{1,0:T(8,128)} async-done(((f32[5120,128]{1,0:T(8,128)}), f32[5120,128]{1,0:T(8,128)}) %all-reduce.4.cloned.1.call-update) | async-done | bytes 2621456 | tf_op jit(solution)/shard_map/psum | solution.py:50
  139.8 0.0 copy-done
  139.8 2.0 subtract_convert_fusion
  141.8 9.7 %fusion.7 = f32[4,1024,128]{1,2,0:T(8,128)S(1)} fusion(bf16[5,4,1024,256]{3,2,1,0:T(8,128)(2,1)} %param.7, bf16[5,1024,128,1]{2,1,0,3:T(8,128)(2,1)S(1)} %bitcast.36, bf16[5,4,1024,256]{3,2,1,0:T(8,128)(2,1)} %param.6, f32[5,4,256]{2,0,1:T(8,128)S(1)} %copy.24), kind=kOutput, calls=%fused_computation.9 | convolution fusion | flops 2685665280 | bytes 24399872 | tf_op jit(solution)/shard_map/ijkr,ijrf->jkf/dot_general | solution.py:55
  151.5 0.0 copy-start.1
  151.5 1.8 copy.26
  153.4 0.0 reduce-scatter.2.cloned.1.call-update
  153.4 31.9 %reduce-scatter.2.cloned.1.call-done = f32[512,128]{1,0:T(8,128)} async-done(((f32[4096,128]{1,0:T(8,128)}), f32[512,128]{1,0:T(8,128)}) %reduce-scatter.2.cloned.1.call-update) | async-done | bytes 262160 | tf_op jit(solution)/shard_map/reduce_scatter | solution.py:57
  185.3 0.0 copy-done.1
  185.3 1.0 sub.43
  186.3 5.6 %collective-permute-start = (f32[1,2,64,128]{3,2,1,0:T(8,128)S(1)}, f32[1,2,64,128]{3,2,1,0:T(8,128)S(1)}, u32[]{:S(2)}, u32[]{:S(2)}) collective-permute-start(f32[1,2,64,128]{3,2,1,0:T(8,128)S(1)} %get-tuple-element.12), channel_id=1, source_target_pairs={{16,0},{32,16},{48,32},{64,48},{80,64},{96,80},{112,96},{17,1},{33... | collective-permute-start | bytes 196616 | tf_op jit(solution)/shard_map/ppermute | solution.py:18
  192.0 1.9 collective-permute-start.1
  193.9 0.0 collective-permute-done
  193.9 1.3 collective-permute-done.1
  195.3 4.5 %collective-permute-start.2 = (f32[6,1,64,128]{3,2,1,0:T(8,128)S(1)}, f32[6,1,64,128]{3,2,1,0:T(8,128)S(1)}, u32[]{:S(2)}, u32[]{:S(2)}) collective-permute-start(f32[6,1,64,128]{3,2,1,0:T(8,128)S(1)} %get-tuple-element.8), channel_id=1, source_target_pairs={{1,0},{2,1},{3,2},{4,3},{5,4},{6,5},{7,6},{8,7},{9,8},{10,9},{11,1... | collective-permute-start | bytes 589832 | tf_op jit(solution)/shard_map/ppermute | solution.py:18
  199.8 1.9 collective-permute-start.3
  201.7 2.3 collective-permute-done.2
  204.0 5.9 %collective-permute-done.3 = f32[6,1,64,128]{3,2,1,0:T(8,128)S(1)} collective-permute-done((f32[6,1,64,128]{3,2,1,0:T(8,128)S(1)}, f32[6,1,64,128]{3,2,1,0:T(8,128)S(1)}, u32[]{:S(2)}, u32[]{:S(2)}) %collective-permute-start.3) | collective-permute-done | bytes 196640 | tf_op jit(solution)/shard_map/ppermute | solution.py:15
  209.9 0.1 select_maximum_fusion.4
  210.0 0.4 multiply_add_fusion.1
  210.5 3.1 %collective-permute-start.4 = (f32[1,2,64,128]{3,2,1,0:T(8,128)S(1)}, f32[1,2,64,128]{3,2,1,0:T(8,128)S(1)}, u32[]{:S(2)}, u32[]{:S(2)}) collective-permute-start(f32[1,2,64,128]{3,2,1,0:T(8,128)S(1)} %get-tuple-element.10), channel_id=1, source_target_pairs={{16,0},{32,16},{48,32},{64,48},{80,64},{96,80},{112,96},{17,1},{33... | collective-permute-start | bytes 196616 | tf_op jit(solution)/shard_map/ppermute | solution.py:18
  213.6 2.9 %collective-permute-start.5 = (f32[1,2,64,128]{3,2,1,0:T(8,128)S(1)}, f32[1,2,64,128]{3,2,1,0:T(8,128)S(1)}, u32[]{:S(2)}, u32[]{:S(2)}) collective-permute-start(f32[1,2,64,128]{3,2,1,0:T(8,128)S(1)} %get-tuple-element.9), channel_id=1, source_target_pairs={{0,16},{16,32},{32,48},{48,64},{64,80},{80,96},{96,112},{1,17},{17... | collective-permute-start | bytes 196616 | tf_op jit(solution)/shard_map/ppermute | solution.py:15
  216.5 0.0 collective-permute-done.4
  216.5 1.3 collective-permute-done.5
  217.9 1.9 collective-permute-start.6
  219.8 3.4 %collective-permute-start.7 = (f32[6,1,64,128]{3,2,1,0:T(8,128)S(1)}, f32[6,1,64,128]{3,2,1,0:T(8,128)S(1)}, u32[]{:S(2)}, u32[]{:S(2)}) collective-permute-start(f32[6,1,64,128]{3,2,1,0:T(8,128)S(1)} %get-tuple-element.5), channel_id=1, source_target_pairs={{0,1},{1,2},{2,3},{3,4},{4,5},{5,6},{6,7},{7,8},{8,9},{9,10},{10,1... | collective-permute-start | bytes 589832 | tf_op jit(solution)/shard_map/ppermute | solution.py:15
  223.2 3.1 %collective-permute-done.6 = f32[6,1,64,128]{3,2,1,0:T(8,128)S(1)} collective-permute-done((f32[6,1,64,128]{3,2,1,0:T(8,128)S(1)}, f32[6,1,64,128]{3,2,1,0:T(8,128)S(1)}, u32[]{:S(2)}, u32[]{:S(2)}) %collective-permute-start.6) | collective-permute-done | bytes 196640 | tf_op jit(solution)/shard_map/ppermute | solution.py:18
  226.2 3.7 %collective-permute-done.7 = f32[6,1,64,128]{3,2,1,0:T(8,128)S(1)} collective-permute-done((f32[6,1,64,128]{3,2,1,0:T(8,128)S(1)}, f32[6,1,64,128]{3,2,1,0:T(8,128)S(1)}, u32[]{:S(2)}, u32[]{:S(2)}) %collective-permute-start.7) | collective-permute-done | bytes 196640 | tf_op jit(solution)/shard_map/ppermute | solution.py:15
  230.0 0.1 select_maximum_fusion
  230.1 1.1 multiply_add_fusion
  (7 shorter events, 0.1 us)
Async XLA Ops:
  6.5 28.7 %all-gather.2.cloned.1.call-start = ((), (), s32[]{:S(2)}) async-start(), calls=%async_computation.1 | async-start | bytes 1179648 | tf_op jit(solution)/shard_map/all_gather | solution.py:40
  8.2 131.6 %all-reduce.4.cloned.1.call-start = ((), (), s32[]{:S(2)}) async-start(), calls=%async_computation.2 | async-start | bytes 5242880 | tf_op jit(solution)/shard_map/psum | solution.py:50
  49.1 90.7 %copy-start = (bf16[5120,128]{1,0:T(8,128)(2,1)S(1)}, bf16[5120,128]{1,0:T(8,128)(2,1)}, u32[]{:S(2)}) copy-start(bf16[5120,128]{1,0:T(8,128)(2,1)} %param.9) | copy-start | bytes 3932164
  49.2 136.2 %reduce-scatter.2.cloned.1.call-start = ((), (), s32[]{:S(2)}) async-start(), calls=%async_computation.3 | async-start | bytes 2359296 | tf_op jit(solution)/shard_map/reduce_scatter | solution.py:57
  151.5 33.8 %copy-start.1 = (f32[4,2,64,128]{3,2,1,0:T(8,128)S(1)}, f32[4,2,64,128]{3,2,1,0:T(8,128)}, u32[]{:S(2)}) copy-start(f32[4,2,64,128]{3,2,1,0:T(8,128)} %param.5) | copy-start | bytes 786436
  186.3 7.6 %collective-permute-start = (f32[1,2,64,128]{3,2,1,0:T(8,128)S(1)}, f32[1,2,64,128]{3,2,1,0:T(8,128)S(1)}, u32[]{:S(2)}, u32[]{:S(2)}) collective-permute-start(f32[1,2,64,128]{3,2,1,0:T(8,128)S(1)} %get-tuple-element.12), channel_id=1, source_target_pairs={{16,0},{32,16},{48,32},{64,48},{80,64},{96,80},{112,96},{17,1},{33... | collective-permute-start | bytes 196616 | tf_op jit(solution)/shard_map/ppermute | solution.py:18
  192.0 3.2 %collective-permute-start.1 = (f32[1,2,64,128]{3,2,1,0:T(8,128)S(1)}, f32[1,2,64,128]{3,2,1,0:T(8,128)S(1)}, u32[]{:S(2)}, u32[]{:S(2)}) collective-permute-start(f32[1,2,64,128]{3,2,1,0:T(8,128)S(1)} %get-tuple-element.11), channel_id=1, source_target_pairs={{0,16},{16,32},{32,48},{48,64},{64,80},{80,96},{96,112},{1,17},{17... | collective-permute-start | bytes 196616 | tf_op jit(solution)/shard_map/ppermute | solution.py:15
  195.3 8.8 %collective-permute-start.2 = (f32[6,1,64,128]{3,2,1,0:T(8,128)S(1)}, f32[6,1,64,128]{3,2,1,0:T(8,128)S(1)}, u32[]{:S(2)}, u32[]{:S(2)}) collective-permute-start(f32[6,1,64,128]{3,2,1,0:T(8,128)S(1)} %get-tuple-element.8), channel_id=1, source_target_pairs={{1,0},{2,1},{3,2},{4,3},{5,4},{6,5},{7,6},{8,7},{9,8},{10,9},{11,1... | collective-permute-start | bytes 589832 | tf_op jit(solution)/shard_map/ppermute | solution.py:18
  199.8 10.1 %collective-permute-start.3 = (f32[6,1,64,128]{3,2,1,0:T(8,128)S(1)}, f32[6,1,64,128]{3,2,1,0:T(8,128)S(1)}, u32[]{:S(2)}, u32[]{:S(2)}) collective-permute-start(f32[6,1,64,128]{3,2,1,0:T(8,128)S(1)} %get-tuple-element.7), channel_id=1, source_target_pairs={{0,1},{1,2},{2,3},{3,4},{4,5},{5,6},{6,7},{7,8},{8,9},{9,10},{10,1... | collective-permute-start | bytes 589832 | tf_op jit(solution)/shard_map/ppermute | solution.py:15
  210.5 6.0 %collective-permute-start.4 = (f32[1,2,64,128]{3,2,1,0:T(8,128)S(1)}, f32[1,2,64,128]{3,2,1,0:T(8,128)S(1)}, u32[]{:S(2)}, u32[]{:S(2)}) collective-permute-start(f32[1,2,64,128]{3,2,1,0:T(8,128)S(1)} %get-tuple-element.10), channel_id=1, source_target_pairs={{16,0},{32,16},{48,32},{64,48},{80,64},{96,80},{112,96},{17,1},{33... | collective-permute-start | bytes 196616 | tf_op jit(solution)/shard_map/ppermute | solution.py:18
  213.6 4.2 %collective-permute-start.5 = (f32[1,2,64,128]{3,2,1,0:T(8,128)S(1)}, f32[1,2,64,128]{3,2,1,0:T(8,128)S(1)}, u32[]{:S(2)}, u32[]{:S(2)}) collective-permute-start(f32[1,2,64,128]{3,2,1,0:T(8,128)S(1)} %get-tuple-element.9), channel_id=1, source_target_pairs={{0,16},{16,32},{32,48},{48,64},{64,80},{80,96},{96,112},{1,17},{17... | collective-permute-start | bytes 196616 | tf_op jit(solution)/shard_map/ppermute | solution.py:15
  217.9 8.4 %collective-permute-start.6 = (f32[6,1,64,128]{3,2,1,0:T(8,128)S(1)}, f32[6,1,64,128]{3,2,1,0:T(8,128)S(1)}, u32[]{:S(2)}, u32[]{:S(2)}) collective-permute-start(f32[6,1,64,128]{3,2,1,0:T(8,128)S(1)} %get-tuple-element.6), channel_id=1, source_target_pairs={{1,0},{2,1},{3,2},{4,3},{5,4},{6,5},{7,6},{8,7},{9,8},{10,9},{11,1... | collective-permute-start | bytes 589832 | tf_op jit(solution)/shard_map/ppermute | solution.py:18
  219.8 10.2 %collective-permute-start.7 = (f32[6,1,64,128]{3,2,1,0:T(8,128)S(1)}, f32[6,1,64,128]{3,2,1,0:T(8,128)S(1)}, u32[]{:S(2)}, u32[]{:S(2)}) collective-permute-start(f32[6,1,64,128]{3,2,1,0:T(8,128)S(1)} %get-tuple-element.5), channel_id=1, source_target_pairs={{0,1},{1,2},{2,3},{3,4},{4,5},{5,6},{6,7},{7,8},{8,9},{9,10},{10,1... | collective-permute-start | bytes 589832 | tf_op jit(solution)/shard_map/ppermute | solution.py:15
Sparse Core Ops, SparseCore 0:
  9.1 26.1 all-gather.1
  49.3 90.4 all-reduce.3
  153.5 31.7 reduce-scatter.1
where the time goes:
time: 238 us
  waiting for transfers between devices  166 us (70%)
  starting transfers between devices  25.4 us (11%)
  matrix products  21.5 us (9%)
  between operations  13.3 us (6%)
  other arithmetic  6.4 us (3%)
  local copies, waits for them, and re-layouts  4.83 us (2%)
    psum x1, waiting for transfers between devices, body(): total = lax.psum(partial_value, 'col')  90.6 us
    reduce_scatter x1, waiting for transfers between devices, body(): lax.psum_scatter(grad_terms, 'row', scatter_dimension=0, tiled=True)  31.9 us
    all_gather x1, waiting for transfers between devices, body(): lax.all_gather(image.astype(jnp.bfloat16), 'row', axis=0, tiled=True)  26.1 us
    ppermute x4, starting transfers between devices, padded_2(): lax.ppermute(lax.slice_in_dim(block, 0, width, axis=dim), axis, backward)  15.2 us
    ppermute x4, waiting for transfers between devices, padded_2(): lax.ppermute(lax.slice_in_dim(block, block.shape[dim] - width, None, axis...  12.2 us
    dot_general x1, matrix products, body(): jnp.einsum('ijkr,ijrf->ikf', u_factors, coef, preferred_element_type=jnp....  11.8 us
    ppermute x4, starting transfers between devices, padded_2(): lax.ppermute(lax.slice_in_dim(block, block.shape[dim] - width, None, axis...  10.1 us
    dot_general x1, matrix products, body(): jnp.einsum('ijkr,ijrf->jkf', v_factors, back, preferred_element_type=jnp....  9.72 us
  transfers between devices with their start and end apart: 11, of which 9 were waited for; matrix products, arithmetic and copies ran while one was open for 0% of the time, Pallas kernels for 0%

commit v1 on v0

--- a/solution.py
+++ b/solution.py
@@ -47,7 +47,9 @@
         "ijkr,ijrf->ikf", u_factors, coef, preferred_element_type=jnp.float32
     )
     partial_value = partial_value.reshape(row_tiles * tile_len, frames)
-    total = lax.psum(partial_value, "col")
+    total = partial_value
+    for hop in (1, 2, 4, 8):
+        total = total + lax.ppermute(total, "col", [(dev, dev ^ hop) for dev in range(16)])
     resid = (total - measured.astype(jnp.float32)).astype(jnp.bfloat16)
     resid = resid.reshape(row_tiles, tile_len, frames)
     back = jnp.einsum("ijkr,ikf->ijrf", u_factors, resid, preferred_element_type=jnp.float32)

time: 238 us -> 382 us (1.61)
  waiting for transfers between devices: 166 us -> 303 us
  starting transfers between devices: 25.4 us -> 31.2 us
    ppermute x0 -> x4, waiting for transfers between devices: none -> 225 us  [body(): lax.ppermute(total, 'col', [(dev, dev ^ hop) for dev in range(16)])]
    psum x1 -> x0, waiting for transfers between devices: 90.6 us -> none  [body(): total = lax.psum(partial_value, 'col')]
    ppermute x0 -> x4, starting transfers between devices: none -> 5.77 us  [body(): lax.ppermute(total, 'col', [(dev, dev ^ hop) for dev in range(16)])]
  transfers between devices with their start and end apart: 11 -> 14, of which waited for: 9 -> 12; matrix products, arithmetic and copies ran while one was open for 0% -> 0% of each run, Pallas kernels for 0% -> 0%
where the time goes in v1:
time: 382 us; the launch traced here: 381 us
  waiting for transfers between devices  303 us (79%)
  starting transfers between devices  31.2 us (8%)
  matrix products  21.5 us (6%)
  between operations  13.6 us (4%)
  other arithmetic  7.5 us (2%)
  local copies, waits for them, and re-layouts  4.8 us (1%)
    ppermute x4, waiting for transfers between devices, body(): lax.ppermute(total, 'col', [(dev, dev ^ hop) for dev in range(16)])  225 us
    reduce_scatter x1, waiting for transfers between devices, body(): lax.psum_scatter(grad_terms, 'row', scatter_dimension=0, tiled=True)  33.7 us
    all_gather x1, waiting for transfers between devices, body(): lax.all_gather(image.astype(jnp.bfloat16), 'row', axis=0, tiled=True)  26.1 us
    ppermute x4, starting transfers between devices, padded_2(): lax.ppermute(lax.slice_in_dim(block, 0, width, axis=dim), axis, backward)  15.3 us
    ppermute x4, waiting for transfers between devices, padded_2(): lax.ppermute(lax.slice_in_dim(block, block.shape[dim] - width, None, axis...  12.2 us
    dot_general x1, matrix products, body(): jnp.einsum('ijkr,ijrf->ikf', u_factors, coef, preferred_element_type=jnp....  11.8 us
    ppermute x4, starting transfers between devices, padded_2(): lax.ppermute(lax.slice_in_dim(block, block.shape[dim] - width, None, axis...  10.1 us
    dot_general x1, matrix products, body(): jnp.einsum('ijkr,ijrf->jkf', v_factors, back, preferred_element_type=jnp....  9.71 us
  transfers between devices with their start and end apart: 14, of which 12 were waited for; matrix products, arithmetic and copies ran while one was open for 0% of the time, Pallas kernels for 0%

profile of v1, /device:TPU:25, one launch (start us, length us, event | category | flops | bytes accessed | tf_op | source)
XLA Modules:
  0.0 381.2 jit_solution(16559150802721427909)
XLA Ops:
  6.5 0.0 all-gather.2.cloned.1.call-start
  6.5 1.6 convert_element_type.28
  8.2 0.0 all-gather.2.cloned.1.call-update
  8.2 0.0 reduce-scatter.2.cloned.1.call-start
  8.2 0.8 copy.20
  9.0 0.1 fusion.25
  9.1 26.1 %all-gather.2.cloned.1.call-done = bf16[32,2,64,128]{3,2,1,0:T(8,128)(2,1)} async-done(((bf16[4,2,64,128]{3,2,1,0:T(8,128)(2,1)}), bf16[32,2,64,128]{3,2,1,0:T(8,128)(2,1)}) %all-gather.2.cloned.1.call-update) | async-done | bytes 1048592 | tf_op jit(solution)/shard_map/all_gather | solution.py:40
  35.2 11.8 %convolution_bitcast_fusion = f32[5,1024,128]{1,2,0:T(8,128)S(1)} fusion(bf16[5,4,1024,256]{3,2,1,0:T(8,128)(2,1)} %param.6, bf16[4,1024,128,1]{2,1,0,3:T(8,128)(2,1)} %bitcast.34, bf16[5,4,1024,256]{3,2,1,0:T(8,128)(2,1)} %param.7, f32[5,4,256]{2,1,0:T(4,128)S(1)} %fusion.25), kind=kOutput, calls=%fused_computation.8 | convolution fusion | flops 2685665280 | bytes 24662016 | tf_op jit(solution)/shard_map/ijkr,ijrf->ikf/dot_general | solution.py:46
  47.0 2.1 copy.21
  49.1 1.2 collective-permute-start
  50.3 57.2 %collective-permute-done = f32[5120,128]{1,0:T(8,128)S(1)} collective-permute-done((f32[5120,128]{1,0:T(8,128)}, f32[5120,128]{1,0:T(8,128)S(1)}, u32[]{:S(2)}, u32[]{:S(2)}) %collective-permute-start) | collective-permute-done | bytes 2621472 | tf_op jit(solution)/shard_map/ppermute | solution.py:52
  107.5 2.1 bitcast_add_fusion
  109.7 2.8 collective-permute-start.1
  112.4 56.1 %collective-permute-done.1 = f32[5120,128]{1,0:T(8,128)S(1)} collective-permute-done((f32[5120,128]{1,0:T(8,128)S(1)}, f32[5120,128]{1,0:T(8,128)S(1)}, u32[]{:S(2)}, u32[]{:S(2)}) %collective-permute-start.1) | collective-permute-done | bytes 2621472 | tf_op jit(solution)/shard_map/ppermute | solution.py:52
  168.5 0.3 add.91
  168.8 0.0 copy-start
  168.8 0.6 collective-permute-start.2
  169.4 55.9 %collective-permute-done.2 = f32[5120,128]{1,0:T(8,128)S(1)} collective-permute-done((f32[5120,128]{1,0:T(8,128)S(1)}, f32[5120,128]{1,0:T(8,128)S(1)}, u32[]{:S(2)}, u32[]{:S(2)}) %collective-permute-start.2) | collective-permute-done | bytes 2621472 | tf_op jit(solution)/shard_map/ppermute | solution.py:52
  225.3 0.4 add.92
  225.7 1.2 collective-permute-start.3
  226.9 55.8 %collective-permute-done.3 = f32[5120,128]{1,0:T(8,128)S(1)} collective-permute-done((f32[5120,128]{1,0:T(8,128)S(1)}, f32[5120,128]{1,0:T(8,128)S(1)}, u32[]{:S(2)}, u32[]{:S(2)}) %collective-permute-start.3) | collective-permute-done | bytes 2621472 | tf_op jit(solution)/shard_map/ppermute | solution.py:52
  282.7 0.0 copy-done
  282.7 0.3 subtract_convert_fusion
  283.1 9.7 %fusion.7 = f32[4,1024,128]{1,2,0:T(8,128)S(1)} fusion(bf16[5,4,1024,256]{3,2,1,0:T(8,128)(2,1)} %param.7, bf16[5,1024,128,1]{2,1,0,3:T(8,128)(2,1)S(1)} %bitcast.37, bf16[5,4,1024,256]{3,2,1,0:T(8,128)(2,1)} %param.6, f32[5,4,256]{2,0,1:T(8,128)S(1)} %copy.24), kind=kOutput, calls=%fused_computation.9 | convolution fusion | flops 2685665280 | bytes 24399872 | tf_op jit(solution)/shard_map/ijkr,ijrf->jkf/dot_general | solution.py:57
  292.8 0.0 copy-start.1
  292.8 1.8 copy.26
  294.6 0.0 reduce-scatter.2.cloned.1.call-update
  294.6 33.7 %reduce-scatter.2.cloned.1.call-done = f32[512,128]{1,0:T(8,128)} async-done(((f32[4096,128]{1,0:T(8,128)}), f32[512,128]{1,0:T(8,128)}) %reduce-scatter.2.cloned.1.call-update) | async-done | bytes 262160 | tf_op jit(solution)/shard_map/reduce_scatter | solution.py:59
  328.4 0.0 copy-done.1
  328.4 1.0 sub.43
  329.4 5.7 %collective-permute-start.4 = (f32[1,2,64,128]{3,2,1,0:T(8,128)S(1)}, f32[1,2,64,128]{3,2,1,0:T(8,128)S(1)}, u32[]{:S(2)}, u32[]{:S(2)}) collective-permute-start(f32[1,2,64,128]{3,2,1,0:T(8,128)S(1)} %get-tuple-element.12), channel_id=1, source_target_pairs={{16,0},{32,16},{48,32},{64,48},{80,64},{96,80},{112,96},{17,1},{33... | collective-permute-start | bytes 196616 | tf_op jit(solution)/shard_map/ppermute | solution.py:18
  335.1 1.9 collective-permute-start.5
  337.0 0.0 collective-permute-done.4
  337.0 1.3 collective-permute-done.5
  338.4 4.6 %collective-permute-start.6 = (f32[6,1,64,128]{3,2,1,0:T(8,128)S(1)}, f32[6,1,64,128]{3,2,1,0:T(8,128)S(1)}, u32[]{:S(2)}, u32[]{:S(2)}) collective-permute-start(f32[6,1,64,128]{3,2,1,0:T(8,128)S(1)} %get-tuple-element.8), channel_id=1, source_target_pairs={{1,0},{2,1},{3,2},{4,3},{5,4},{6,5},{7,6},{8,7},{9,8},{10,9},{11,1... | collective-permute-start | bytes 589832 | tf_op jit(solution)/shard_map/ppermute | solution.py:18
  343.0 1.9 collective-permute-start.7
  344.9 2.3 collective-permute-done.6
  347.2 5.9 %collective-permute-done.7 = f32[6,1,64,128]{3,2,1,0:T(8,128)S(1)} collective-permute-done((f32[6,1,64,128]{3,2,1,0:T(8,128)S(1)}, f32[6,1,64,128]{3,2,1,0:T(8,128)S(1)}, u32[]{:S(2)}, u32[]{:S(2)}) %collective-permute-start.7) | collective-permute-done | bytes 196640 | tf_op jit(solution)/shard_map/ppermute | solution.py:15
  353.1 0.1 select_maximum_fusion.4
  353.2 0.4 multiply_add_fusion.1
  353.6 3.1 collective-permute-start.8
  356.7 2.9 collective-permute-start.9
  359.6 0.0 collective-permute-done.8
  359.7 1.3 collective-permute-done.9
  361.0 1.9 collective-permute-start.10
  363.0 3.4 collective-permute-start.11
  366.3 3.1 collective-permute-done.10
  369.4 3.7 collective-permute-done.11
  373.1 0.1 select_maximum_fusion
  373.2 1.1 multiply_add_fusion
  (7 shorter events, 0.1 us)
Async XLA Ops:
  6.5 28.7 %all-gather.2.cloned.1.call-start = ((), (), s32[]{:S(2)}) async-start(), calls=%async_computation.1 | async-start | bytes 1179648 | tf_op jit(solution)/shard_map/all_gather | solution.py:40
  8.2 320.2 %reduce-scatter.2.cloned.1.call-start = ((), (), s32[]{:S(2)}) async-start(), calls=%async_computation.2 | async-start | bytes 2359296 | tf_op jit(solution)/shard_map/reduce_scatter | solution.py:59
  49.1 58.4 %collective-permute-start = (f32[5120,128]{1,0:T(8,128)}, f32[5120,128]{1,0:T(8,128)S(1)}, u32[]{:S(2)}, u32[]{:S(2)}) collective-permute-start(f32[5120,128]{1,0:T(8,128)} %bitcast.35), channel_id=1, source_target_pairs={{0,1},{1,0},{2,3},{3,2},{4,5},{5,4},{6,7},{7,6},{8,9},{9,8},{10,11... | collective-permute-start | bytes 7864328 | tf_op jit(solution)/shard_map/ppermute | solution.py:52
  109.7 58.9 %collective-permute-start.1 = (f32[5120,128]{1,0:T(8,128)S(1)}, f32[5120,128]{1,0:T(8,128)S(1)}, u32[]{:S(2)}, u32[]{:S(2)}) collective-permute-start(f32[5120,128]{1,0:T(8,128)S(1)} %bitcast_add_fusion), channel_id=1, source_target_pairs={{0,2},{1,3},{2,0},{3,1},{4,6},{5,7},{6,4},{7,5},{8,10},{9,11},{10,... | collective-permute-start | bytes 7864328 | tf_op jit(solution)/shard_map/ppermute | solution.py:52
  168.8 113.9 %copy-start = (bf16[5120,128]{1,0:T(8,128)(2,1)S(1)}, bf16[5120,128]{1,0:T(8,128)(2,1)}, u32[]{:S(2)}) copy-start(bf16[5120,128]{1,0:T(8,128)(2,1)} %param.9) | copy-start | bytes 3932164
  168.8 56.5 %collective-permute-start.2 = (f32[5120,128]{1,0:T(8,128)S(1)}, f32[5120,128]{1,0:T(8,128)S(1)}, u32[]{:S(2)}, u32[]{:S(2)}) collective-permute-start(f32[5120,128]{1,0:T(8,128)S(1)} %add.91), channel_id=1, source_target_pairs={{0,4},{1,5},{2,6},{3,7},{4,0},{5,1},{6,2},{7,3},{8,12},{9,13},{10,... | collective-permute-start | bytes 7864328 | tf_op jit(solution)/shard_map/ppermute | solution.py:52
  225.7 57.0 %collective-permute-start.3 = (f32[5120,128]{1,0:T(8,128)S(1)}, f32[5120,128]{1,0:T(8,128)S(1)}, u32[]{:S(2)}, u32[]{:S(2)}) collective-permute-start(f32[5120,128]{1,0:T(8,128)S(1)} %add.92), channel_id=1, source_target_pairs={{0,8},{1,9},{2,10},{3,11},{4,12},{5,13},{6,14},{7,15},{8,0},{9,1},... | collective-permute-start | bytes 7864328 | tf_op jit(solution)/shard_map/ppermute | solution.py:52
  292.8 35.6 %copy-start.1 = (f32[4,2,64,128]{3,2,1,0:T(8,128)S(1)}, f32[4,2,64,128]{3,2,1,0:T(8,128)}, u32[]{:S(2)}) copy-start(f32[4,2,64,128]{3,2,1,0:T(8,128)} %param.5) | copy-start | bytes 786436
  329.4 7.6 %collective-permute-start.4 = (f32[1,2,64,128]{3,2,1,0:T(8,128)S(1)}, f32[1,2,64,128]{3,2,1,0:T(8,128)S(1)}, u32[]{:S(2)}, u32[]{:S(2)}) collective-permute-start(f32[1,2,64,128]{3,2,1,0:T(8,128)S(1)} %get-tuple-element.12), channel_id=1, source_target_pairs={{16,0},{32,16},{48,32},{64,48},{80,64},{96,80},{112,96},{17,1},{33... | collective-permute-start | bytes 196616 | tf_op jit(solution)/shard_map/ppermute | solution.py:18
  335.1 3.2 collective-permute-start.5
  338.4 8.8 %collective-permute-start.6 = (f32[6,1,64,128]{3,2,1,0:T(8,128)S(1)}, f32[6,1,64,128]{3,2,1,0:T(8,128)S(1)}, u32[]{:S(2)}, u32[]{:S(2)}) collective-permute-start(f32[6,1,64,128]{3,2,1,0:T(8,128)S(1)} %get-tuple-element.8), channel_id=1, source_target_pairs={{1,0},{2,1},{3,2},{4,3},{5,4},{6,5},{7,6},{8,7},{9,8},{10,9},{11,1... | collective-permute-start | bytes 589832 | tf_op jit(solution)/shard_map/ppermute | solution.py:18
  343.0 10.1 %collective-permute-start.7 = (f32[6,1,64,128]{3,2,1,0:T(8,128)S(1)}, f32[6,1,64,128]{3,2,1,0:T(8,128)S(1)}, u32[]{:S(2)}, u32[]{:S(2)}) collective-permute-start(f32[6,1,64,128]{3,2,1,0:T(8,128)S(1)} %get-tuple-element.7), channel_id=1, source_target_pairs={{0,1},{1,2},{2,3},{3,4},{4,5},{5,6},{6,7},{7,8},{8,9},{9,10},{10,1... | collective-permute-start | bytes 589832 | tf_op jit(solution)/shard_map/ppermute | solution.py:15
  353.6 6.0 %collective-permute-start.8 = (f32[1,2,64,128]{3,2,1,0:T(8,128)S(1)}, f32[1,2,64,128]{3,2,1,0:T(8,128)S(1)}, u32[]{:S(2)}, u32[]{:S(2)}) collective-permute-start(f32[1,2,64,128]{3,2,1,0:T(8,128)S(1)} %get-tuple-element.10), channel_id=1, source_target_pairs={{16,0},{32,16},{48,32},{64,48},{80,64},{96,80},{112,96},{17,1},{33... | collective-permute-start | bytes 196616 | tf_op jit(solution)/shard_map/ppermute | solution.py:18
  356.7 4.2 %collective-permute-start.9 = (f32[1,2,64,128]{3,2,1,0:T(8,128)S(1)}, f32[1,2,64,128]{3,2,1,0:T(8,128)S(1)}, u32[]{:S(2)}, u32[]{:S(2)}) collective-permute-start(f32[1,2,64,128]{3,2,1,0:T(8,128)S(1)} %get-tuple-element.9), channel_id=1, source_target_pairs={{0,16},{16,32},{32,48},{48,64},{64,80},{80,96},{96,112},{1,17},{17... | collective-permute-start | bytes 196616 | tf_op jit(solution)/shard_map/ppermute | solution.py:15
  361.0 8.4 %collective-permute-start.10 = (f32[6,1,64,128]{3,2,1,0:T(8,128)S(1)}, f32[6,1,64,128]{3,2,1,0:T(8,128)S(1)}, u32[]{:S(2)}, u32[]{:S(2)}) collective-permute-start(f32[6,1,64,128]{3,2,1,0:T(8,128)S(1)} %get-tuple-element.6), channel_id=1, source_target_pairs={{1,0},{2,1},{3,2},{4,3},{5,4},{6,5},{7,6},{8,7},{9,8},{10,9},{11,1... | collective-permute-start | bytes 589832 | tf_op jit(solution)/shard_map/ppermute | solution.py:18
  363.0 10.2 %collective-permute-start.11 = (f32[6,1,64,128]{3,2,1,0:T(8,128)S(1)}, f32[6,1,64,128]{3,2,1,0:T(8,128)S(1)}, u32[]{:S(2)}, u32[]{:S(2)}) collective-permute-start(f32[6,1,64,128]{3,2,1,0:T(8,128)S(1)} %get-tuple-element.5), channel_id=1, source_target_pairs={{0,1},{1,2},{2,3},{3,4},{4,5},{5,6},{6,7},{7,8},{8,9},{9,10},{10,1... | collective-permute-start | bytes 589832 | tf_op jit(solution)/shard_map/ppermute | solution.py:15
Sparse Core Ops, SparseCore 0:
  9.1 26.1 all-gather.1
  294.8 33.5 reduce-scatter.1
